TPU v7x, 32 devices: a whole 2x2x4 slice. The times are simulated.
32 devices in a mesh: groups: 2 (over y), expert: 4 (over z), sub: 4 (over x, core).
Axes of the slice: x: 2, y: 2, z: 4, core: 2. Of those that a mesh axis runs over, the one named last changes fastest.
Arguments:
- tokens: bfloat16 [512, 7168], P(('groups', 'expert', 'sub')), parts along dimension 0, may hold values from -6 to 6
- route_ids: int32 [512, 2], P(('groups', 'expert', 'sub')), parts along dimension 0, may hold values from 0 to 3, all different within a row; in each aligned block of 16 rows (0 to 15, 16 to 31, ...) at most 12 rows name the same one
- weight_index: int32 [512, 2], P(('groups', 'expert', 'sub')), parts along dimension 0, may hold values from 0 to 63
- combine_table: float32 [64], replicated, may hold values from 0.05 to 1
- w_gate: bfloat16 [4, 7168, 1024], P('expert', None, 'sub'), may hold values from -0.0625 to 0.0625
- w_up: bfloat16 [4, 7168, 1024], P('expert', None, 'sub'), may hold values from -0.0625 to 0.0625
- w_down: bfloat16 [4, 1024, 7168], P('expert', 'sub'), may hold values from -0.1875 to 0.1875
Outputs:
- mixed: bfloat16 [512, 7168], P(('groups', 'expert', 'sub')), parts along dimension 0
There are 2 independent parts, one for each index of `groups`. A program takes and returns all parts, laid end to end along the dimension named above; an argument that names none is the same for every part. Nothing has to cross between parts.
Inputs may be any that keep to these rules, and one draw needn't show every extreme that they name: `route_ids`: each row names 2 different experts; among the 16 rows of one device no expert is named by more than 12 of them, a bound that some block reaches.
All inputs are finite; a program needn't handle non-finite values.
Results may differ from a plain program's by a relative error of at most 0.013.
Values may be sent and summed in bfloat16 or wider, within the bound.
A program may use at most 128 MiB of HBM per device.

v0:
```python
import jax
import jax.numpy as jnp
from jax import lax
from jax.sharding import PartitionSpec as P


def expert_partial(rows_in, w_gate, w_up, w_down):
    gate = jnp.dot(rows_in, w_gate[0], preferred_element_type=jnp.float32)
    upper = jnp.dot(rows_in, w_up[0], preferred_element_type=jnp.float32)
    hidden = (jax.nn.silu(gate) * upper).astype(jnp.bfloat16)
    return jnp.dot(hidden, w_down[0], preferred_element_type=jnp.float32)


def shards(tokens, route_ids, weight_index, combine_table, w_gate, w_up, w_down):
    n_expert = lax.axis_size("expert")
    n_rows, n_width = tokens.shape
    topk = route_ids.shape[1]
    capacity = max(n_rows * topk * 3 // (2 * n_expert), n_rows * topk // n_expert + 2)
    slots_all = n_expert * capacity
    flat_ids = route_ids.reshape(-1)
    onehot = (flat_ids[:, None] == jnp.arange(n_expert, dtype=jnp.int32)[None, :]).astype(jnp.int32)
    earlier = jnp.cumsum(onehot, axis=0) - onehot
    slot = jnp.sum(earlier * onehot, axis=1)
    target = (flat_ids * capacity + slot).reshape(n_rows, topk)
    positions = jnp.arange(slots_all, dtype=jnp.int32)
    select = jnp.any(target[None, :, :] == positions[:, None, None], axis=2)
    send_rows = jnp.dot(
        select.astype(jnp.bfloat16), tokens, preferred_element_type=jnp.float32
    ).astype(jnp.bfloat16)
    landed = lax.all_to_all(send_rows, "expert", split_axis=0, concat_axis=0, tiled=True)
    gathered = lax.all_gather(landed, "sub", axis=0, tiled=True)
    summed = lax.psum_scatter(
        expert_partial(gathered, w_gate, w_up, w_down).astype(jnp.bfloat16),
        "sub",
        scatter_dimension=0,
        tiled=True,
    )
    returned = lax.all_to_all(summed, "expert", split_axis=0, concat_axis=0, tiled=True)
    table_size = combine_table.shape[0]
    weights = jnp.sum(
        jnp.where(
            weight_index[:, :, None] == jnp.arange(table_size, dtype=jnp.int32)[None, None, :],
            combine_table[None, None, :],
            0.0,
        ),
        axis=2,
    )
    mixing = jnp.sum(
        jnp.where(target[:, :, None] == positions[None, None, :], weights[:, :, None], 0.0), axis=1
    )
    total = jnp.dot(mixing, returned.astype(jnp.float32), precision=lax.Precision.HIGHEST)
    return (2.5 * total / jnp.sum(weights, axis=1)[:, None]).astype(jnp.bfloat16)


def solution(mesh):
    return jax.shard_map(
        shards,
        mesh=mesh,
        in_specs=(
            P(("groups", "expert", "sub"), None),
            P(("groups", "expert", "sub"), None),
            P(("groups", "expert", "sub"), None),
            P(),
            P("expert", None, "sub"),
            P("expert", None, "sub"),
            P("expert", "sub", None),
        ),
        out_specs=P(("groups", "expert", "sub"), None),
        check_vma=False,
    )
```

profile of v0, /device:TPU:0, one launch (start us, length us, event | category | flops | bytes accessed | tf_op | source)
XLA Modules:
  0.0 150.1 jit_solution(17152920133590119091)
XLA Ops:
  6.5 0.0 copy-start
  6.5 0.0 all-gather.2.cloned.1.call-start
  6.5 0.8 copy.21
  7.3 0.1 eq.26
  7.4 0.1 fusion.21
  7.5 0.1 reduce_window_sum.11
  7.6 0.2 select_reduce_fusion.3
  7.7 0.1 reduce_sum.39
  7.8 0.1 copy.22
  7.9 0.7 multiply_add_fusion
  8.6 0.1 fusion.22
  8.7 0.0 copy-done
  8.7 0.4 convolution_convert_fusion.1
  9.1 0.2 all_to_all.16
  9.3 29.0 %all_to_all.24 = bf16[4,12,7168]{2,1,0:T(8,128)(2,1)S(1)} all-to-all(bf16[4,12,7168]{2,1,0:T(8,128)(2,1)S(1)} %all_to_all.16), channel_id=1, replica_groups=mesh['groups'=2,'expert'=4,'sub'=4] {'expert'}, dimensions={0} | all-to-all | bytes 1376256 | tf_op jit(solution)/shard_map/all_to_all | solution.py:30
  38.3 1.0 all_to_all.18
  39.3 0.0 all-gather.2.cloned.1.call-update
  39.3 0.0 reduce-scatter.2.cloned.1.call-start
  39.4 25.5 %all-gather.2.cloned.1.call-done = bf16[192,7168]{1,0:T(8,128)(2,1)} async-done(((bf16[48,7168]{1,0:T(8,128)(2,1)}), bf16[192,7168]{1,0:T(8,128)(2,1)}) %all-gather.2.cloned.1.call-update) | async-done | bytes 2752528 | tf_op jit(solution)/shard_map/all_gather | solution.py:31
  64.9 3.9 %fusion.5 = f32[192,256]{1,0:T(8,128)S(1)} fusion(bf16[192,7168]{1,0:T(8,128)(2,1)} %all-gather.2.cloned.1.call-done, bf16[1,7168,256]{2,1,0:T(8,128)(2,1)} %param.11), kind=kOutput, calls=%fused_computation.8 | convolution fusion | flops 704643072 | bytes 6619136 | tf_op jit(solution)/shard_map/dot_general | solution.py:8
  68.8 0.0 copy-done.1
  68.8 7.8 %convolution_convert_fusion = bf16[192,7168]{1,0:T(8,128)(2,1)} fusion(bf16[1,256,7168]{2,1,0:T(8,128)(2,1)} %param.13, bf16[192,7168]{1,0:T(8,128)(2,1)S(1)} %copy-done.1, bf16[1,7168,256]{2,1,0:T(8,128)(2,1)} %param.12, f32[192,256]{1,0:T(8,128)S(1)} %fusion.5), kind=kOutput, calls=%fused_computation | convolution fusion | flops 1410957312 | bytes 13041664 | tf_op jit(solution)/shard_map/dot_general | solution.py:11
  76.6 0.0 reduce-scatter.2.cloned.1.call-update
  76.6 35.6 %reduce-scatter.2.cloned.1.call-done = bf16[48,7168]{1,0:T(8,128)(2,1)} async-done(((bf16[192,7168]{1,0:T(8,128)(2,1)}), bf16[48,7168]{1,0:T(8,128)(2,1)}) %reduce-scatter.2.cloned.1.call-update) | async-done | bytes 688144 | tf_op jit(solution)/shard_map/reduce_scatter | solution.py:32
  112.2 2.2 %all_to_all.19 = bf16[4,12,7168]{2,1,0:T(8,128)(2,1)} reshape(bf16[48,7168]{1,0:T(8,128)(2,1)} %reduce-scatter.2.cloned.1.call-done) | data formatting | bytes 1376256 | tf_op jit(solution)/shard_map/all_to_all | solution.py:38
  114.4 4.6 %all-to-all-start.1 = ((bf16[4,12,7168]{2,1,0:T(8,128)(2,1)}), bf16[4,12,7168]{2,1,0:T(8,128)(2,1)S(1)}, u32[]{:S(2)}, u32[]{:S(2)}) async-start(bf16[4,12,7168]{2,1,0:T(8,128)(2,1)} %all_to_all.19), calls=%async_computation.2 | async-start | bytes 1835008 | tf_op jit(solution)/shard_map/all_to_all | solution.py:38
  119.0 0.0 copy-done.2
  119.0 0.2 select_reduce_fusion
  119.2 0.1 select_reduce_fusion.2
  119.3 22.6 %all-to-all-done.1 = bf16[4,12,7168]{2,1,0:T(8,128)(2,1)S(1)} async-done(((bf16[4,12,7168]{2,1,0:T(8,128)(2,1)}), bf16[4,12,7168]{2,1,0:T(8,128)(2,1)S(1)}, u32[]{:S(2)}, u32[]{:S(2)}) %all-to-all-start.1) | async-done | bytes 688160 | tf_op jit(solution)/shard_map/all_to_all | solution.py:38
  142.0 0.2 all_to_all.21
  142.1 1.1 fusion.1
  (4 shorter events, 0.0 us)
Async XLA Ops:
  6.5 2.2 %copy-start = (bf16[16,7168]{1,0:T(8,128)(2,1)S(1)}, bf16[16,7168]{1,0:T(8,128)(2,1)}, u32[]{:S(2)}) copy-start(bf16[16,7168]{1,0:T(8,128)(2,1)} %param.7) | copy-start | bytes 688132
  6.5 58.4 %all-gather.2.cloned.1.call-start = ((), (), s32[]{:S(2)}) async-start(), calls=%async_computation.3 | async-start | bytes 3440640 | tf_op jit(solution)/shard_map/all_gather | solution.py:31
  39.3 72.9 %reduce-scatter.2.cloned.1.call-start = ((), (), s32[]{:S(2)}) async-start(), calls=%async_computation.4 | async-start | bytes 3440640 | tf_op jit(solution)/shard_map/reduce_scatter | solution.py:32
  64.9 3.9 %copy-start.1 = (bf16[192,7168]{1,0:T(8,128)(2,1)S(1)}, bf16[192,7168]{1,0:T(8,128)(2,1)}, u32[]{:S(2)}) copy-start(bf16[192,7168]{1,0:T(8,128)(2,1)} %all-gather.2.cloned.1.call-done) | copy-start | bytes 8257540
  76.6 42.4 %copy-start.2 = (s32[16,2]{0,1:T(2,128)S(1)}, s32[16,2]{0,1:T(2,128)}, u32[]{:S(2)}) copy-start(s32[16,2]{0,1:T(2,128)} %param.9) | copy-start | bytes 388
  76.6 42.4 %copy-start.3 = (f32[64]{0:T(128)S(1)}, f32[64]{0:T(128)}, u32[]{:S(2)}) copy-start(f32[64]{0:T(128)} %param.10) | copy-start | bytes 772
  114.4 27.5 %all-to-all-start.1 = ((bf16[4,12,7168]{2,1,0:T(8,128)(2,1)}), bf16[4,12,7168]{2,1,0:T(8,128)(2,1)S(1)}, u32[]{:S(2)}, u32[]{:S(2)}) async-start(bf16[4,12,7168]{2,1,0:T(8,128)(2,1)} %all_to_all.19), calls=%async_computation.2 | async-start | bytes 1835008 | tf_op jit(solution)/shard_map/all_to_all | solution.py:38
Sparse Core Ops, SparseCore 0:
  39.5 25.3 all-gather.1
  76.7 35.4 reduce-scatter.1
where the time goes:
time: 150 us
  waiting for transfers between devices  83.8 us (56%)
  blocking collectives  29 us (19%)
  between operations  13.5 us (9%)
  matrix products  13.2 us (9%)
  starting transfers between devices  4.64 us (3%)
  local copies, waits for them, and re-layouts  4.61 us (3%)
    reduce_scatter x1, waiting for transfers between devices, shards(): lax.psum_scatter(expert_partial(gathered, w_gate, w_up, w_down).astype(jn...  35.6 us
    all_to_all x1, blocking collectives, shards(): lax.all_to_all(send_rows, 'expert', split_axis=0, concat_axis=0, tiled=True)  29 us
    all_gather x1, waiting for transfers between devices, shards(): gathered = lax.all_gather(landed, 'sub', axis=0, tiled=True)  25.5 us
    all_to_all x1, waiting for transfers between devices, shards(): lax.all_to_all(summed, 'expert', split_axis=0, concat_axis=0, tiled=True)  22.6 us
    dot_general x1, matrix products, expert_partial(): return jnp.dot(hidden, w_down[0], preferred_element_type=jnp.float32)  7.79 us
    all_to_all x1, starting transfers between devices, shards(): lax.all_to_all(summed, 'expert', split_axis=0, concat_axis=0, tiled=True)  4.6 us
    dot_general x1, matrix products, expert_partial(): gate = jnp.dot(rows_in, w_gate[0], preferred_element_type=jnp.float32)  3.89 us
  transfers between devices with their start and end apart: 3, of which 3 were waited for; matrix products, arithmetic and copies ran while one was open for 0% of the time, Pallas kernels for 0%

commit v1 on v0

--- a/solution.py
+++ b/solution.py
@@ -1,7 +1,330 @@
+import functools
+
 import jax
 import jax.numpy as jnp
 from jax import lax
+from jax.experimental import pallas as pl
+from jax.experimental.pallas import tpu as pltpu
 from jax.sharding import PartitionSpec as P
+
+MESH = pl.DeviceIdType.MESH
+EXTRA = 128
+HALF = 64
+
+
+def order_of(place, n, step):
+    both = jnp.minimum(place, n - 1 - place)
+    far = (step + 1) // 2
+    near = jnp.where(step % 2 == 1, place - far, place + far)
+    rest = jnp.where(place < n - 1 - place, step, n - 1 - step)
+    return jnp.where(step <= 2 * both, near, rest)
+
+
+def coefficients(ids, index, table, n_expert):
+    rows, topk = ids.shape
+    lane = lax.broadcasted_iota(jnp.int32, (rows, EXTRA), 1)
+    entry = lax.broadcasted_iota(jnp.int32, (rows, table.shape[1]), 1)
+    named = jnp.zeros((rows, EXTRA), jnp.float32)
+    total = jnp.zeros((rows, 1), jnp.float32)
+    for k in range(topk):
+        weight = jnp.sum(jnp.where(entry == index[:, k : k + 1], table, 0.0), axis=1, keepdims=True)
+        named += jnp.where(lane % HALF == ids[:, k : k + 1], weight, 0.0)
+        total += weight
+    factor = 2.5 * named / total
+    high = factor.astype(jnp.bfloat16)
+    low = (factor - high.astype(jnp.float32)).astype(jnp.bfloat16)
+    return jnp.where(lane < HALF, high.astype(jnp.float32), low.astype(jnp.float32)).astype(jnp.bfloat16)
+
+
+def kernel(
+    n, tok_ref, ids_ref, index_ref, table_ref, wg_hbm, wu_hbm, wd_hbm, out_ref,
+    rows_buf, wg, wu, wd, part, core_in, x_out, x_in, z_out, z_right, z_left,
+    w_sem, tok_sem,
+    zr_send, zl_send, z_recv, xa_send, xa_recv, ca_send, ca_recv, cb_send, cb_recv,
+    c_send, c_recv, x_send, x_recv, r_send, r_recv, l_send, l_recv,
+):
+    me = lax.axis_index("expert")
+    sub = lax.axis_index("sub")
+    cross, core = sub // 2, sub % 2
+    other_core = {"sub": cross * 2 + 1 - core}
+    other_x = {"sub": (1 - cross) * 2 + core}
+    width = tok_ref.shape[1]
+    nr = tok_ref.shape[0]
+
+    copies_w = [
+        pltpu.make_async_copy(wg_hbm.at[0], wg, w_sem.at[0]),
+        pltpu.make_async_copy(wu_hbm.at[0], wu, w_sem.at[1]),
+        pltpu.make_async_copy(wd_hbm.at[0], wd, w_sem.at[2]),
+    ]
+
+    def place(c, x):
+        return pl.ds(pl.multiple_of((c * 2 + x) * nr, nr), nr)
+
+    mine = place(core, cross)
+    copy_tok = pltpu.make_async_copy(tok_ref, rows_buf.at[me, mine, pl.ds(0, width)], tok_sem)
+    copy_tok.start()
+
+    barrier = pltpu.get_barrier_semaphore()
+    pl.semaphore_signal(barrier, inc=1, device_id=other_core, device_id_type=MESH)
+    pl.semaphore_signal(barrier, inc=1, device_id=other_x, device_id_type=MESH)
+
+    @pl.when(me > 0)
+    def _():
+        pl.semaphore_signal(barrier, inc=1, device_id={"expert": me - 1}, device_id_type=MESH)
+
+    @pl.when(me < n - 1)
+    def _():
+        pl.semaphore_signal(barrier, inc=1, device_id={"expert": me + 1}, device_id_type=MESH)
+
+    rows_buf[me, mine, pl.ds(width, EXTRA)] = coefficients(
+        ids_ref[...], index_ref[...], table_ref[...], n
+    )
+    peers = 2 + jnp.where(me > 0, 1, 0) + jnp.where(me < n - 1, 1, 0)
+    pl.semaphore_wait(barrier, peers)
+    copy_tok.wait()
+
+    def remote(src, dst, send, recv, device):
+        return pltpu.make_async_remote_copy(
+            src_ref=src, dst_ref=dst, send_sem=send, recv_sem=recv,
+            device_id=device, device_id_type=MESH,
+        )
+
+    def to_right(b):
+        ref = rows_buf.at[b, mine]
+        return remote(ref, ref, zr_send.at[b], z_recv.at[b], {"expert": me + 1})
+
+    def to_left(b):
+        ref = rows_buf.at[b, mine]
+        return remote(ref, ref, zl_send.at[b], z_recv.at[b], {"expert": me - 1})
+
+    def across(b):
+        ref = rows_buf.at[b, mine]
+        return remote(ref, ref, xa_send.at[b], xa_recv.at[b], other_x)
+
+    def beside(b):
+        ref = rows_buf.at[b, mine]
+        return remote(ref, ref, ca_send.at[b], ca_recv.at[b], other_core)
+
+    def beside_far(b):
+        ref = rows_buf.at[b, place(core, 1 - cross)]
+        return remote(ref, ref, cb_send.at[b], cb_recv.at[b], other_core)
+
+    def part_beside(b):
+        return remote(
+            part.at[b, pl.ds(pl.multiple_of((1 - core) * 2 * nr, nr), 2 * nr)],
+            core_in.at[b], c_send.at[b], c_recv.at[b], other_core,
+        )
+
+    def part_across(b):
+        return remote(x_out.at[b], x_in.at[b], x_send.at[b], x_recv.at[b], other_x)
+
+    def part_right(b):
+        return remote(z_out.at[b], z_right.at[b], r_send.at[b], r_recv.at[b], {"expert": me + 1})
+
+    def part_left(b):
+        return remote(z_out.at[b], z_left.at[b], l_send.at[b], l_recv.at[b], {"expert": me - 1})
+
+    def spread(b):
+        @pl.when((b <= me) & (me < n - 1))
+        def _():
+            to_right(b).start()
+
+        @pl.when((b >= me) & (me > 0))
+        def _():
+            to_left(b).start()
+
+        across(b).start()
+        beside(b).start()
+
+    spread(me)
+    for copy in copies_w:
+        copy.start()
+    for copy in copies_w:
+        copy.wait()
+
+    depth = 1024
+
+    def compute(b):
+        gate = jnp.zeros((4 * nr, wg.shape[1]), jnp.float32)
+        upper = jnp.zeros((4 * nr, wg.shape[1]), jnp.float32)
+        for k in range(0, width, depth):
+            piece = rows_buf[b, :, k : k + depth]
+            gate += jnp.dot(piece, wg[k : k + depth, :], preferred_element_type=jnp.float32)
+            upper += jnp.dot(piece, wu[k : k + depth, :], preferred_element_type=jnp.float32)
+        extra = rows_buf[b, :, width : width + EXTRA].astype(jnp.float32)
+        lane = lax.broadcasted_iota(jnp.int32, extra.shape, 1)
+        factor = jnp.sum(jnp.where(lane % HALF == me, extra, 0.0), axis=1, keepdims=True)
+        hidden = (gate / (1.0 + jnp.exp(-gate)) * upper * factor).astype(jnp.bfloat16)
+        for k in range(0, width, depth):
+            part[b, :, k : k + depth] = jnp.dot(
+                hidden, wd[:, k : k + depth], preferred_element_type=jnp.float32
+            ).astype(jnp.bfloat16)
+
+    def gather_step(k, carry):
+        @pl.when(k < n)
+        def _():
+            b = order_of(me, n, k)
+            to_right(b).wait_recv()
+            spread(b)
+
+        b = order_of(me, n, k - 1)
+        across(b).wait_recv()
+        beside_far(b).start()
+        beside(b).wait_recv()
+        beside_far(b).wait_recv()
+        compute(b)
+        part_beside(b).start()
+        return carry
+
+    lax.fori_loop(1, n + 1, gather_step, 0)
+
+    far_rows = pl.ds(pl.multiple_of((1 - cross) * nr, nr), nr)
+    own_rows = pl.ds(pl.multiple_of(cross * nr, nr), nr)
+
+    def cross_step(k, carry):
+        b = order_of(me, n, n - 1 - k)
+        part_beside(b).wait_recv()
+        x_out[b] = (
+            part[b, place(core, 1 - cross)].astype(jnp.float32)
+            + core_in[b, far_rows].astype(jnp.float32)
+        ).astype(jnp.bfloat16)
+        part_across(b).start()
+        return carry
+
+    lax.fori_loop(0, n, cross_step, 0)
+
+    def reduced(b):
+        return (
+            part[b, mine].astype(jnp.float32)
+            + core_in[b, own_rows].astype(jnp.float32)
+            + x_in[b].astype(jnp.float32)
+        )
+
+    def return_step(k, carry):
+        b = order_of(me, n, n - 1 - k)
+        part_across(b).wait_recv()
+
+        @pl.when(b > me)
+        def _():
+            @pl.when(me > 0)
+            def _():
+                part_right(b).wait_recv()
+                z_out[b] = (reduced(b) + z_right[b].astype(jnp.float32)).astype(jnp.bfloat16)
+
+            @pl.when(me == 0)
+            def _():
+                z_out[b] = reduced(b).astype(jnp.bfloat16)
+
+            part_right(b).start()
+
+        @pl.when(b < me)
+        def _():
+            @pl.when(me < n - 1)
+            def _():
+                part_left(b).wait_recv()
+                z_out[b] = (reduced(b) + z_left[b].astype(jnp.float32)).astype(jnp.bfloat16)
+
+            @pl.when(me == n - 1)
+            def _():
+                z_out[b] = reduced(b).astype(jnp.bfloat16)
+
+            part_left(b).start()
+
+        return carry
+
+    lax.fori_loop(0, n - 1, return_step, 0)
+
+    part_across(me).wait_recv()
+
+    @pl.when(me > 0)
+    def _():
+        part_right(me).wait_recv()
+
+    @pl.when(me < n - 1)
+    def _():
+        part_left(me).wait_recv()
+
+    @pl.when(me == 0)
+    def _():
+        out_ref[...] = (reduced(me) + z_left[me].astype(jnp.float32)).astype(jnp.bfloat16)
+
+    @pl.when(me == n - 1)
+    def _():
+        out_ref[...] = (reduced(me) + z_right[me].astype(jnp.float32)).astype(jnp.bfloat16)
+
+    @pl.when((me > 0) & (me < n - 1))
+    def _():
+        out_ref[...] = (
+            reduced(me) + z_left[me].astype(jnp.float32) + z_right[me].astype(jnp.float32)
+        ).astype(jnp.bfloat16)
+
+    def finish(b, carry):
+        @pl.when((b <= me) & (me < n - 1))
+        def _():
+            to_right(b).wait_send()
+
+        @pl.when((b >= me) & (me > 0))
+        def _():
+            to_left(b).wait_send()
+
+        across(b).wait_send()
+        beside(b).wait_send()
+        beside_far(b).wait_send()
+        part_beside(b).wait_send()
+        part_across(b).wait_send()
+
+        @pl.when(b > me)
+        def _():
+            part_right(b).wait_send()
+
+        @pl.when(b < me)
+        def _():
+            part_left(b).wait_send()
+
+        return carry
+
+    lax.fori_loop(0, n, finish, 0)
+
+
+def fused(tokens, route_ids, weight_index, combine_table, w_gate, w_up, w_down):
+    n = lax.axis_size("expert")
+    rows, width = tokens.shape
+    units = w_gate.shape[2]
+    group = 4 * rows
+    bf16 = jnp.bfloat16
+    vmem = pl.BlockSpec(memory_space=pltpu.VMEM)
+    hbm = pl.BlockSpec(memory_space=pl.ANY)
+    dma = pltpu.SemaphoreType.DMA
+    block = pltpu.VMEM((n, rows, width), bf16)
+    return pl.pallas_call(
+        functools.partial(kernel, n),
+        out_shape=jax.ShapeDtypeStruct((rows, width), bf16),
+        in_specs=[hbm, vmem, vmem, vmem, hbm, hbm, hbm],
+        out_specs=vmem,
+        scratch_shapes=[
+            pltpu.VMEM((n, group, width + EXTRA), bf16),
+            pltpu.VMEM((width, units), bf16),
+            pltpu.VMEM((width, units), bf16),
+            pltpu.VMEM((units, width), bf16),
+            pltpu.VMEM((n, group, width), bf16),
+            pltpu.VMEM((n, 2 * rows, width), bf16),
+            block, block, block, block, block,
+            dma((3,)), dma,
+        ] + [dma((n,))] * 17,
+        compiler_params=pltpu.CompilerParams(
+            collective_id=0, has_side_effects=True, vmem_limit_bytes=56 * 2**20
+        ),
+    )(tokens, route_ids, weight_index, combine_table[None, :], w_gate, w_up, w_down)
+
+
+def fits(tokens, w_gate):
+    n, subs = lax.axis_size("expert"), lax.axis_size("sub")
+    rows, width = tokens.shape
+    held = n * rows * 15 + 3 * w_gate.shape[2]
+    return (
+        subs == 4 and 1 < n <= HALF and rows % 16 == 0 and width % 1024 == 0
+        and held * width * 2 <= 44 * 2**20
+    )
 
 
 def expert_partial(rows_in, w_gate, w_up, w_down):
@@ -12,6 +335,8 @@
 
 
 def shards(tokens, route_ids, weight_index, combine_table, w_gate, w_up, w_down):
+    if fits(tokens, w_gate):
+        return fused(tokens, route_ids, weight_index, combine_table, w_gate, w_up, w_down)
     n_expert = lax.axis_size("expert")
     n_rows, n_width = tokens.shape
     topk = route_ids.shape[1]

time: 150 us -> 69.2 us (0.46)
  waiting for transfers between devices: 83.8 us -> 0 us
  Pallas kernels: 0 us -> 64.6 us
  blocking collectives: 29 us -> 0 us
  between operations: 13.5 us -> 0.01 us
  matrix products: 13.2 us -> 0 us
  starting transfers between devices: 4.64 us -> 0 us
    pallas_call x0 -> x1, Pallas kernels: none -> 64.6 us  [fused(): pl.pallas_call(functools.partial(kernel, n), out_shape=jax.ShapeDtypeStru...]
    reduce_scatter x1 -> x0, waiting for transfers between devices: 35.6 us -> none  [shards(): lax.psum_scatter(expert_partial(gathered, w_gate, w_up, w_down).astype(jn...]
    all_to_all x1 -> x0, blocking collectives: 29 us -> none  [shards(): lax.all_to_all(send_rows, 'expert', split_axis=0, concat_axis=0, tiled=True)]
    all_gather x1 -> x0, waiting for transfers between devices: 25.5 us -> none  [shards(): gathered = lax.all_gather(landed, 'sub', axis=0, tiled=True)]
    all_to_all x1 -> x0, waiting for transfers between devices: 22.6 us -> none  [shards(): lax.all_to_all(summed, 'expert', split_axis=0, concat_axis=0, tiled=True)]
    dot_general x4 -> x0, matrix products: 13.2 us -> none  [the longest x1 7.79 us: expert_partial(): return jnp.dot(hidden, w_down[0], preferred_element_type=jnp.float32)]
    all_to_all x1 -> x0, starting transfers between devices: 4.6 us -> none  [shards(): lax.all_to_all(summed, 'expert', split_axis=0, concat_axis=0, tiled=True)]
    all_to_all x4 -> x0, local copies, waits for them, and re-layouts: 3.54 us -> none  [the longest x2 2.36 us: shards(): lax.all_to_all(summed, 'expert', split_axis=0, concat_axis=0, tiled=True)]
  transfers between devices with their start and end apart: 3 -> 0, of which waited for: 3 -> 0; matrix products, arithmetic and copies ran while one was open for 0% -> 0% of each run, Pallas kernels for 0% -> 0%
where the time goes in v1:
time: 69.2 us; the launch traced here: 68.9 us
  Pallas kernels  64.6 us (93%)
  local copies, waits for them, and re-layouts  4.34 us (6%)
    pallas_call x1, Pallas kernels, fused(): pl.pallas_call(functools.partial(kernel, n), out_shape=jax.ShapeDtypeStru...  64.6 us
    unnamed x3, local copies, waits for them, and re-layouts  4.34 us

profile of v1, /device:TPU:0, one launch (start us, length us, event | category | flops | bytes accessed | tf_op | source)
XLA Modules:
  0.0 68.9 jit_solution(16903205719874741686)
XLA Ops:
  0.0 1.4 %copy.8.ids_ref = s32[16,2]{1,0:T(8,128)} copy(s32[16,2]{0,1:T(2,128)} %param.8) | data formatting | bytes 256 | tf_op args[1]
  1.4 1.4 %copy.9.index_ref = s32[16,2]{1,0:T(8,128)} copy(s32[16,2]{0,1:T(2,128)} %param.9) | data formatting | bytes 256 | tf_op args[2]
  2.7 64.6 %shard_map.73 = bf16[16,7168]{1,0:T(8,128)(2,1)} custom-call(bf16[16,7168]{1,0:T(8,128)(2,1)} %tok_ref.1, s32[16,2]{1,0:T(8,128)} %copy.8.ids_ref, s32[16,2]{1,0:T(8,128)} %copy.9.index_ref, f32[1,64]{1,0:T(1,128)} %bitcast.1, bf16[1,7168,256]{2,1,0:T(8,128)(2,1)} %wg_hbm.1, bf16[1,7168,256]{2,1,0:T(8,128)(2,1)} %wu_hbm.1, bf16[1,256,7168]{2,1,0:T(8,128)(2,1)} %wd_hbm.1), custom_call_target="tpu_custom_call" | custom-call | tf_op jit(solution)/shard_map/pallas_call | solution.py:299
  67.3 1.6 %copy.11 = bf16[16,7168]{1,0:T(8,128)(2,1)} copy(bf16[16,7168]{1,0:T(8,128)(2,1)} %shard_map.73) | data formatting | bytes 458752

commit v2 on v1

--- a/solution.py
+++ b/solution.py
@@ -10,25 +10,36 @@
 MESH = pl.DeviceIdType.MESH
 EXTRA = 128
 HALF = 64
+CUTS = 2
+AHEAD = 2
 
 
 def order_of(place, n, step):
     both = jnp.minimum(place, n - 1 - place)
     far = (step + 1) // 2
-    near = jnp.where(step % 2 == 1, place - far, place + far)
-    rest = jnp.where(place < n - 1 - place, step, n - 1 - step)
+    left = place < n - 1 - place
+    near = jnp.where((step % 2 == 1) == left, place - far, place + far)
+    rest = jnp.where(left, step, n - 1 - step)
     return jnp.where(step <= 2 * both, near, rest)
 
 
-def coefficients(ids, index, table, n_expert):
-    rows, topk = ids.shape
+def column(row):
+    size = row.shape[1]
+    spot = lax.broadcasted_iota(jnp.int32, (size, size), 0)
+    same = spot == lax.broadcasted_iota(jnp.int32, (size, size), 1)
+    picked = jnp.where(same, row.astype(jnp.float32), 0.0)
+    return jnp.sum(picked, axis=1, keepdims=True).astype(jnp.int32)
+
+
+def coefficients(ids, index, table):
+    topk, rows = ids.shape
     lane = lax.broadcasted_iota(jnp.int32, (rows, EXTRA), 1)
     entry = lax.broadcasted_iota(jnp.int32, (rows, table.shape[1]), 1)
     named = jnp.zeros((rows, EXTRA), jnp.float32)
     total = jnp.zeros((rows, 1), jnp.float32)
     for k in range(topk):
-        weight = jnp.sum(jnp.where(entry == index[:, k : k + 1], table, 0.0), axis=1, keepdims=True)
-        named += jnp.where(lane % HALF == ids[:, k : k + 1], weight, 0.0)
+        weight = jnp.sum(jnp.where(entry == column(index[k : k + 1, :]), table, 0.0), axis=1, keepdims=True)
+        named += jnp.where(lane % HALF == column(ids[k : k + 1, :]), weight, 0.0)
         total += weight
     factor = 2.5 * named / total
     high = factor.astype(jnp.bfloat16)
@@ -63,6 +74,8 @@
     mine = place(core, cross)
     copy_tok = pltpu.make_async_copy(tok_ref, rows_buf.at[me, mine, pl.ds(0, width)], tok_sem)
     copy_tok.start()
+    for copy in copies_w:
+        copy.start()
 
     barrier = pltpu.get_barrier_semaphore()
     pl.semaphore_signal(barrier, inc=1, device_id=other_core, device_id_type=MESH)
@@ -77,7 +90,7 @@
         pl.semaphore_signal(barrier, inc=1, device_id={"expert": me + 1}, device_id_type=MESH)
 
     rows_buf[me, mine, pl.ds(width, EXTRA)] = coefficients(
-        ids_ref[...], index_ref[...], table_ref[...], n
+        ids_ref[...], index_ref[...], table_ref[...]
     )
     peers = 2 + jnp.where(me > 0, 1, 0) + jnp.where(me < n - 1, 1, 0)
     pl.semaphore_wait(barrier, peers)
@@ -89,59 +102,63 @@
             device_id=device, device_id_type=MESH,
         )
 
-    def to_right(b):
-        ref = rows_buf.at[b, mine]
-        return remote(ref, ref, zr_send.at[b], z_recv.at[b], {"expert": me + 1})
-
-    def to_left(b):
-        ref = rows_buf.at[b, mine]
-        return remote(ref, ref, zl_send.at[b], z_recv.at[b], {"expert": me - 1})
-
-    def across(b):
-        ref = rows_buf.at[b, mine]
-        return remote(ref, ref, xa_send.at[b], xa_recv.at[b], other_x)
-
-    def beside(b):
-        ref = rows_buf.at[b, mine]
-        return remote(ref, ref, ca_send.at[b], ca_recv.at[b], other_core)
-
-    def beside_far(b):
-        ref = rows_buf.at[b, place(core, 1 - cross)]
-        return remote(ref, ref, cb_send.at[b], cb_recv.at[b], other_core)
-
-    def part_beside(b):
+    half = width // CUTS
+
+    def cols(h):
+        return pl.ds(h * half, half + (EXTRA if h == CUTS - 1 else 0))
+
+    def cut(h):
+        return pl.ds(h * half, half)
+
+    def to_right(b, h):
+        ref = rows_buf.at[b, mine, cols(h)]
+        return remote(ref, ref, zr_send.at[b, h], z_recv.at[b, h], {"expert": me + 1})
+
+    def to_left(b, h):
+        ref = rows_buf.at[b, mine, cols(h)]
+        return remote(ref, ref, zl_send.at[b, h], z_recv.at[b, h], {"expert": me - 1})
+
+    def across(b, h):
+        ref = rows_buf.at[b, mine, cols(h)]
+        return remote(ref, ref, xa_send.at[b, h], xa_recv.at[b, h], other_x)
+
+    def beside(b, h):
+        ref = rows_buf.at[b, mine, cols(h)]
+        return remote(ref, ref, ca_send.at[b, h], ca_recv.at[b, h], other_core)
+
+    def beside_far(b, h):
+        ref = rows_buf.at[b, place(core, 1 - cross), cols(h)]
+        return remote(ref, ref, cb_send.at[b, h], cb_recv.at[b, h], other_core)
+
+    def part_beside(b, h):
         return remote(
-            part.at[b, pl.ds(pl.multiple_of((1 - core) * 2 * nr, nr), 2 * nr)],
-            core_in.at[b], c_send.at[b], c_recv.at[b], other_core,
+            part.at[b, pl.ds(pl.multiple_of((1 - core) * 2 * nr, nr), 2 * nr), cut(h)],
+            core_in.at[b, :, cut(h)], c_send.at[b, h], c_recv.at[b, h], other_core,
         )
 
-    def part_across(b):
-        return remote(x_out.at[b], x_in.at[b], x_send.at[b], x_recv.at[b], other_x)
-
-    def part_right(b):
-        return remote(z_out.at[b], z_right.at[b], r_send.at[b], r_recv.at[b], {"expert": me + 1})
-
-    def part_left(b):
-        return remote(z_out.at[b], z_left.at[b], l_send.at[b], l_recv.at[b], {"expert": me - 1})
-
-    def spread(b):
+    def part_across(b, h):
+        return remote(x_out.at[b, :, cut(h)], x_in.at[b, :, cut(h)], x_send.at[b, h], x_recv.at[b, h], other_x)
+
+    def part_right(b, h):
+        return remote(z_out.at[b, :, cut(h)], z_right.at[b, :, cut(h)], r_send.at[b, h], r_recv.at[b, h], {"expert": me + 1})
+
+    def part_left(b, h):
+        return remote(z_out.at[b, :, cut(h)], z_left.at[b, :, cut(h)], l_send.at[b, h], l_recv.at[b, h], {"expert": me - 1})
+
+    def spread(b, h):
         @pl.when((b <= me) & (me < n - 1))
         def _():
-            to_right(b).start()
+            to_right(b, h).start()
 
         @pl.when((b >= me) & (me > 0))
         def _():
-            to_left(b).start()
-
-        across(b).start()
-        beside(b).start()
-
-    spread(me)
-    for copy in copies_w:
-        copy.start()
-    for copy in copies_w:
-        copy.wait()
-
+            to_left(b, h).start()
+
+        across(b, h).start()
+        beside(b, h).start()
+
+    for h in range(CUTS):
+        spread(me, h)
     depth = 1024
 
     def compute(b):
@@ -155,131 +172,160 @@
         lane = lax.broadcasted_iota(jnp.int32, extra.shape, 1)
         factor = jnp.sum(jnp.where(lane % HALF == me, extra, 0.0), axis=1, keepdims=True)
         hidden = (gate / (1.0 + jnp.exp(-gate)) * upper * factor).astype(jnp.bfloat16)
-        for k in range(0, width, depth):
-            part[b, :, k : k + depth] = jnp.dot(
-                hidden, wd[:, k : k + depth], preferred_element_type=jnp.float32
-            ).astype(jnp.bfloat16)
+        step = half // 4
+        for h in range(CUTS):
+            for k in range(h * half, (h + 1) * half, step):
+                part[b, :, k : k + step] = jnp.dot(
+                    hidden, wd[:, k : k + step], preferred_element_type=jnp.float32
+                ).astype(jnp.bfloat16)
+            part_beside(b, h).start()
+
+    far_rows = pl.ds(pl.multiple_of((1 - cross) * nr, nr), nr)
+    own_rows = pl.ds(pl.multiple_of(cross * nr, nr), nr)
+
+    def give_across(b, h):
+        part_beside(b, h).wait_recv()
+        x_out[b, :, cut(h)] = (
+            part[b, place(core, 1 - cross), cut(h)].astype(jnp.float32)
+            + core_in[b, far_rows, cut(h)].astype(jnp.float32)
+        ).astype(jnp.bfloat16)
+        part_across(b, h).start()
 
     def gather_step(k, carry):
         @pl.when(k < n)
         def _():
             b = order_of(me, n, k)
-            to_right(b).wait_recv()
-            spread(b)
+            for h in range(CUTS):
+                to_right(b, h).wait_recv()
+                spread(b, h)
 
         b = order_of(me, n, k - 1)
-        across(b).wait_recv()
-        beside_far(b).start()
-        beside(b).wait_recv()
-        beside_far(b).wait_recv()
+        for h in range(CUTS):
+            across(b, h).wait_recv()
+            beside_far(b, h).start()
+
+        @pl.when(k == 1)
+        def _():
+            for copy in copies_w:
+                copy.wait()
+
+        @pl.when(k == n)
+        def _():
+            for h in range(CUTS):
+                give_across(order_of(me, n, n - 2), h)
+
+        for h in range(CUTS):
+            beside(b, h).wait_recv()
+            beside_far(b, h).wait_recv()
         compute(b)
-        part_beside(b).start()
         return carry
 
     lax.fori_loop(1, n + 1, gather_step, 0)
 
-    far_rows = pl.ds(pl.multiple_of((1 - cross) * nr, nr), nr)
-    own_rows = pl.ds(pl.multiple_of(cross * nr, nr), nr)
-
-    def cross_step(k, carry):
-        b = order_of(me, n, n - 1 - k)
-        part_beside(b).wait_recv()
-        x_out[b] = (
-            part[b, place(core, 1 - cross)].astype(jnp.float32)
-            + core_in[b, far_rows].astype(jnp.float32)
-        ).astype(jnp.bfloat16)
-        part_across(b).start()
-        return carry
-
-    lax.fori_loop(0, n, cross_step, 0)
-
-    def reduced(b):
+    back = [order_of(me, n, n - 1 - k) for k in range(n)]
+    waiting = [(back[k], h) for k in range(n) if k != 1 for h in range(CUTS)]
+
+    def next_across():
+        if waiting:
+            give_across(*waiting.pop(0))
+
+    for _ in range(AHEAD):
+        next_across()
+
+    def reduced(b, h):
         return (
-            part[b, mine].astype(jnp.float32)
-            + core_in[b, own_rows].astype(jnp.float32)
-            + x_in[b].astype(jnp.float32)
+            part[b, mine, cut(h)].astype(jnp.float32)
+            + core_in[b, own_rows, cut(h)].astype(jnp.float32)
+            + x_in[b, :, cut(h)].astype(jnp.float32)
         )
 
-    def return_step(k, carry):
-        b = order_of(me, n, n - 1 - k)
-        part_across(b).wait_recv()
-
-        @pl.when(b > me)
-        def _():
-            @pl.when(me > 0)
-            def _():
-                part_right(b).wait_recv()
-                z_out[b] = (reduced(b) + z_right[b].astype(jnp.float32)).astype(jnp.bfloat16)
-
-            @pl.when(me == 0)
-            def _():
-                z_out[b] = reduced(b).astype(jnp.bfloat16)
-
-            part_right(b).start()
-
-        @pl.when(b < me)
-        def _():
-            @pl.when(me < n - 1)
-            def _():
-                part_left(b).wait_recv()
-                z_out[b] = (reduced(b) + z_left[b].astype(jnp.float32)).astype(jnp.bfloat16)
-
-            @pl.when(me == n - 1)
-            def _():
-                z_out[b] = reduced(b).astype(jnp.bfloat16)
-
-            part_left(b).start()
-
-        return carry
-
-    lax.fori_loop(0, n - 1, return_step, 0)
-
-    part_across(me).wait_recv()
-
-    @pl.when(me > 0)
-    def _():
-        part_right(me).wait_recv()
-
-    @pl.when(me < n - 1)
-    def _():
-        part_left(me).wait_recv()
-
-    @pl.when(me == 0)
-    def _():
-        out_ref[...] = (reduced(me) + z_left[me].astype(jnp.float32)).astype(jnp.bfloat16)
-
-    @pl.when(me == n - 1)
-    def _():
-        out_ref[...] = (reduced(me) + z_right[me].astype(jnp.float32)).astype(jnp.bfloat16)
-
-    @pl.when((me > 0) & (me < n - 1))
-    def _():
-        out_ref[...] = (
-            reduced(me) + z_left[me].astype(jnp.float32) + z_right[me].astype(jnp.float32)
-        ).astype(jnp.bfloat16)
+    for k in (1, 0, *range(2, n - 1)):
+        b = back[k]
+        for h in range(CUTS):
+            part_across(b, h).wait_recv()
+            if k != 1:
+                next_across()
+
+            @pl.when(b > me)
+            def _():
+                @pl.when(me > 0)
+                def _():
+                    part_right(b, h).wait_recv()
+                    z_out[b, :, cut(h)] = (
+                        reduced(b, h) + z_right[b, :, cut(h)].astype(jnp.float32)
+                    ).astype(jnp.bfloat16)
+
+                @pl.when(me == 0)
+                def _():
+                    z_out[b, :, cut(h)] = reduced(b, h).astype(jnp.bfloat16)
+
+                part_right(b, h).start()
+
+            @pl.when(b < me)
+            def _():
+                @pl.when(me < n - 1)
+                def _():
+                    part_left(b, h).wait_recv()
+                    z_out[b, :, cut(h)] = (
+                        reduced(b, h) + z_left[b, :, cut(h)].astype(jnp.float32)
+                    ).astype(jnp.bfloat16)
+
+                @pl.when(me == n - 1)
+                def _():
+                    z_out[b, :, cut(h)] = reduced(b, h).astype(jnp.bfloat16)
+
+                part_left(b, h).start()
+
+    for h in range(CUTS):
+        part_across(me, h).wait_recv()
+
+        @pl.when(me == 0)
+        def _():
+            part_left(me, h).wait_recv()
+            out_ref[:, cut(h)] = (
+                reduced(me, h) + z_left[me, :, cut(h)].astype(jnp.float32)
+            ).astype(jnp.bfloat16)
+
+        @pl.when(me == n - 1)
+        def _():
+            part_right(me, h).wait_recv()
+            out_ref[:, cut(h)] = (
+                reduced(me, h) + z_right[me, :, cut(h)].astype(jnp.float32)
+            ).astype(jnp.bfloat16)
+
+        @pl.when((me > 0) & (me < n - 1))
+        def _():
+            part_right(me, h).wait_recv()
+            part_left(me, h).wait_recv()
+            out_ref[:, cut(h)] = (
+                reduced(me, h)
+                + z_left[me, :, cut(h)].astype(jnp.float32)
+                + z_right[me, :, cut(h)].astype(jnp.float32)
+            ).astype(jnp.bfloat16)
 
     def finish(b, carry):
-        @pl.when((b <= me) & (me < n - 1))
-        def _():
-            to_right(b).wait_send()
-
-        @pl.when((b >= me) & (me > 0))
-        def _():
-            to_left(b).wait_send()
-
-        across(b).wait_send()
-        beside(b).wait_send()
-        beside_far(b).wait_send()
-        part_beside(b).wait_send()
-        part_across(b).wait_send()
-
-        @pl.when(b > me)
-        def _():
-            part_right(b).wait_send()
-
-        @pl.when(b < me)
-        def _():
-            part_left(b).wait_send()
+        for h in range(CUTS):
+            @pl.when((b <= me) & (me < n - 1))
+            def _():
+                to_right(b, h).wait_send()
+
+            @pl.when((b >= me) & (me > 0))
+            def _():
+                to_left(b, h).wait_send()
+
+            across(b, h).wait_send()
+            beside(b, h).wait_send()
+            beside_far(b, h).wait_send()
+            part_beside(b, h).wait_send()
+            part_across(b, h).wait_send()
+
+            @pl.when(b > me)
+            def _():
+                part_right(b, h).wait_send()
+
+            @pl.when(b < me)
+            def _():
+                part_left(b, h).wait_send()
 
         return carry
 
@@ -310,11 +356,11 @@
             pltpu.VMEM((n, 2 * rows, width), bf16),
             block, block, block, block, block,
             dma((3,)), dma,
-        ] + [dma((n,))] * 17,
+        ] + [dma((n, CUTS))] * 17,
         compiler_params=pltpu.CompilerParams(
             collective_id=0, has_side_effects=True, vmem_limit_bytes=56 * 2**20
         ),
-    )(tokens, route_ids, weight_index, combine_table[None, :], w_gate, w_up, w_down)
+    )(tokens, route_ids.T, weight_index.T, combine_table[None, :], w_gate, w_up, w_down)
 
 
 def fits(tokens, w_gate):
@@ -322,7 +368,7 @@
     rows, width = tokens.shape
     held = n * rows * 15 + 3 * w_gate.shape[2]
     return (
-        subs == 4 and 1 < n <= HALF and rows % 16 == 0 and width % 1024 == 0
+        subs == 4 and n == 4 and rows % 16 == 0 and width % 1024 == 0
         and held * width * 2 <= 44 * 2**20
     )
 

time: 69.2 us -> 63 us (0.910)
  Pallas kernels: 64.6 us -> 61.2 us
  local copies, waits for them, and re-layouts: 4.34 us -> 1.64 us
    pallas_call x1, Pallas kernels: 64.6 us -> 61.2 us  [fused(): pl.pallas_call(functools.partial(kernel, n), out_shape=jax.ShapeDtypeStru...]
    unnamed x3 -> x1, local copies, waits for them, and re-layouts: 4.34 us -> 1.64 us
where the time goes in v2:
time: 63 us; the launch traced here: 62.8 us
  Pallas kernels  61.2 us (97%)
  local copies, waits for them, and re-layouts  1.64 us (3%)
    pallas_call x1, Pallas kernels, fused(): pl.pallas_call(functools.partial(kernel, n), out_shape=jax.ShapeDtypeStru...  61.2 us
    unnamed x1, local copies, waits for them, and re-layouts  1.64 us

profile of v2, /device:TPU:0, one launch (start us, length us, event | category | flops | bytes accessed | tf_op | source)
XLA Modules:
  0.0 62.8 jit_solution(3256449908208422601)
XLA Ops:
  0.0 61.2 %shard_map.73 = bf16[16,7168]{1,0:T(8,128)(2,1)} custom-call(bf16[16,7168]{1,0:T(8,128)(2,1)} %tok_ref.1, s32[2,16]{1,0:T(2,128)} %bitcast.3, s32[2,16]{1,0:T(2,128)} %bitcast.4, f32[1,64]{1,0:T(1,128)} %bitcast.5, bf16[1,7168,256]{2,1,0:T(8,128)(2,1)} %wg_hbm.1, bf16[1,7168,256]{2,1,0:T(8,128)(2,1)} %wu_hbm.1, bf16[1,256,7168]{2,1,0:T(8,128)(2,1)} %wd_hbm.1), custom_call_target="tpu_custom_call" | custom-call | tf_op jit(solution)/shard_map/pallas_call | solution.py:345
  61.2 1.6 %copy.9 = bf16[16,7168]{1,0:T(8,128)(2,1)} copy(bf16[16,7168]{1,0:T(8,128)(2,1)} %shard_map.73) | data formatting | bytes 458752

commit v3 on v2

--- a/solution.py
+++ b/solution.py
@@ -159,15 +159,18 @@
 
     for h in range(CUTS):
         spread(me, h)
-    depth = 1024
+    depth = half // 2
 
     def compute(b):
         gate = jnp.zeros((4 * nr, wg.shape[1]), jnp.float32)
         upper = jnp.zeros((4 * nr, wg.shape[1]), jnp.float32)
-        for k in range(0, width, depth):
-            piece = rows_buf[b, :, k : k + depth]
-            gate += jnp.dot(piece, wg[k : k + depth, :], preferred_element_type=jnp.float32)
-            upper += jnp.dot(piece, wu[k : k + depth, :], preferred_element_type=jnp.float32)
+        for h in range(CUTS):
+            beside(b, h).wait_recv()
+            beside_far(b, h).wait_recv()
+            for k in range(h * half, (h + 1) * half, depth):
+                piece = rows_buf[b, :, k : k + depth]
+                gate += jnp.dot(piece, wg[k : k + depth, :], preferred_element_type=jnp.float32)
+                upper += jnp.dot(piece, wu[k : k + depth, :], preferred_element_type=jnp.float32)
         extra = rows_buf[b, :, width : width + EXTRA].astype(jnp.float32)
         lane = lax.broadcasted_iota(jnp.int32, extra.shape, 1)
         factor = jnp.sum(jnp.where(lane % HALF == me, extra, 0.0), axis=1, keepdims=True)
@@ -214,9 +217,6 @@
             for h in range(CUTS):
                 give_across(order_of(me, n, n - 2), h)
 
-        for h in range(CUTS):
-            beside(b, h).wait_recv()
-            beside_far(b, h).wait_recv()
         compute(b)
         return carry
 

time: 63 us -> 63.6 us (level)
  no operation moved by 1% of the time
where the time goes in v3:
time: 63.6 us; the launch traced here: 63.4 us
  Pallas kernels  61.8 us (97%)
  local copies, waits for them, and re-layouts  1.64 us (3%)
    pallas_call x1, Pallas kernels, fused(): pl.pallas_call(functools.partial(kernel, n), out_shape=jax.ShapeDtypeStru...  61.8 us
    unnamed x1, local copies, waits for them, and re-layouts  1.64 us

profile of v3, /device:TPU:0, one launch (start us, length us, event | category | flops | bytes accessed | tf_op | source)
XLA Modules:
  0.0 63.4 jit_solution(1460903639815131787)
XLA Ops:
  0.0 61.8 %shard_map.73 = bf16[16,7168]{1,0:T(8,128)(2,1)} custom-call(bf16[16,7168]{1,0:T(8,128)(2,1)} %tok_ref.1, s32[2,16]{1,0:T(2,128)} %bitcast.3, s32[2,16]{1,0:T(2,128)} %bitcast.4, f32[1,64]{1,0:T(1,128)} %bitcast.5, bf16[1,7168,256]{2,1,0:T(8,128)(2,1)} %wg_hbm.1, bf16[1,7168,256]{2,1,0:T(8,128)(2,1)} %wu_hbm.1, bf16[1,256,7168]{2,1,0:T(8,128)(2,1)} %wd_hbm.1), custom_call_target="tpu_custom_call" | custom-call | tf_op jit(solution)/shard_map/pallas_call | solution.py:345
  61.8 1.6 %copy.9 = bf16[16,7168]{1,0:T(8,128)(2,1)} copy(bf16[16,7168]{1,0:T(8,128)(2,1)} %shard_map.73) | data formatting | bytes 458752

commit v4 on v2

--- a/solution.py
+++ b/solution.py
@@ -284,14 +284,14 @@
             part_left(me, h).wait_recv()
             out_ref[:, cut(h)] = (
                 reduced(me, h) + z_left[me, :, cut(h)].astype(jnp.float32)
-            ).astype(jnp.bfloat16)
+            )
 
         @pl.when(me == n - 1)
         def _():
             part_right(me, h).wait_recv()
             out_ref[:, cut(h)] = (
                 reduced(me, h) + z_right[me, :, cut(h)].astype(jnp.float32)
-            ).astype(jnp.bfloat16)
+            )
 
         @pl.when((me > 0) & (me < n - 1))
         def _():
@@ -301,7 +301,7 @@
                 reduced(me, h)
                 + z_left[me, :, cut(h)].astype(jnp.float32)
                 + z_right[me, :, cut(h)].astype(jnp.float32)
-            ).astype(jnp.bfloat16)
+            )
 
     def finish(b, carry):
         for h in range(CUTS):
@@ -344,7 +344,7 @@
     block = pltpu.VMEM((n, rows, width), bf16)
     return pl.pallas_call(
         functools.partial(kernel, n),
-        out_shape=jax.ShapeDtypeStruct((rows, width), bf16),
+        out_shape=jax.ShapeDtypeStruct((rows, width), jnp.float32),
         in_specs=[hbm, vmem, vmem, vmem, hbm, hbm, hbm],
         out_specs=vmem,
         scratch_shapes=[
@@ -360,7 +360,7 @@
         compiler_params=pltpu.CompilerParams(
             collective_id=0, has_side_effects=True, vmem_limit_bytes=56 * 2**20
         ),
-    )(tokens, route_ids.T, weight_index.T, combine_table[None, :], w_gate, w_up, w_down)
+    )(tokens, route_ids.T, weight_index.T, combine_table[None, :], w_gate, w_up, w_down).astype(bf16)
 
 
 def fits(tokens, w_gate):

time: 63 us -> 63.2 us (level)
  other arithmetic: 0 us -> 1.73 us
  local copies, waits for them, and re-layouts: 1.64 us -> 0 us
    convert_element_type x0 -> x1, other arithmetic: none -> 1.73 us  [fused(): return pl.pallas_call(functools.partial(kernel, n), out_shape=jax.ShapeDt...]
    unnamed x1 -> x0, local copies, waits for them, and re-layouts: 1.64 us -> none
where the time goes in v4:
time: 63.2 us; the launch traced here: 63 us
  Pallas kernels  61.3 us (97%)
  other arithmetic  1.73 us (3%)
    pallas_call x1, Pallas kernels, fused(): pl.pallas_call(functools.partial(kernel, n), out_shape=jax.ShapeDtypeStru...  61.3 us
    convert_element_type x1, other arithmetic, fused(): return pl.pallas_call(functools.partial(kernel, n), out_shape=jax.ShapeDt...  1.73 us

profile of v4, /device:TPU:0, one launch (start us, length us, event | category | flops | bytes accessed | tf_op | source)
XLA Modules:
  0.0 63.0 jit_solution(10441912259933875415)
XLA Ops:
  0.0 61.3 %shard_map.73 = f32[16,7168]{1,0:T(8,128)} custom-call(bf16[16,7168]{1,0:T(8,128)(2,1)} %tok_ref.1, s32[2,16]{1,0:T(2,128)} %bitcast.3, s32[2,16]{1,0:T(2,128)} %bitcast.4, f32[1,64]{1,0:T(1,128)} %bitcast.5, bf16[1,7168,256]{2,1,0:T(8,128)(2,1)} %wg_hbm.1, bf16[1,7168,256]{2,1,0:T(8,128)(2,1)} %wu_hbm.1, bf16[1,256,7168]{2,1,0:T(8,128)(2,1)} %wd_hbm.1), custom_call_target="tpu_custom_call" | custom-call | tf_op jit(solution)/shard_map/pallas_call | solution.py:345
  61.3 1.7 %convert_element_type.3 = bf16[16,7168]{1,0:T(8,128)(2,1)} convert(f32[16,7168]{1,0:T(8,128)} %shard_map.73) | non-fusion elementwise | flops 114688 | bytes 688128 | tf_op jit(solution)/shard_map/convert_element_type | solution.py:363
